TPU v7x, 128 devices: a whole 4x4x4 slice. The times are simulated.
128 devices in a mesh: dp: 32 (over z, x, core), db: 4 (over y).
Axes of the slice: x: 4, y: 4, z: 4, core: 2. Of those that a mesh axis runs over, the one named last changes fastest.
Arguments:
- queries: bfloat16 [18432, 4096], P('dp', 'db'), may hold values from -100 to 100
- cotangent: bfloat16 [18432, 4096], P('dp', 'db'), may hold values from -6 to 6
- db_states: bfloat16 [1024, 128, 896], P('dp', 'db'), may hold values from -6 to 6
- key_weight: bfloat16 [896, 4096], P(None, 'db'), may hold values from -0.1875 to 0.1875
- value_weight: bfloat16 [896, 4096], P(None, 'db'), may hold values from -0.1875 to 0.1875
- conv_kernel: float32 [3, 896], replicated, may hold values from -2.5 to 2.5
- nbr_owner: int32 [288, 2], P('dp'), may hold values from 0 to 31, all different within a row; in each aligned block of 9 rows (0 to 8, 9 to 17, ...) at most 2 rows name the same one
- nbr_row: int32 [288, 2], P('dp'), may hold values from 0 to 31
Outputs:
- attended: bfloat16 [18432, 4096], P('dp', 'db')
- grad_queries: bfloat16 [18432, 4096], P('dp', 'db')
- grad_states: float32 [1024, 128, 896], P('dp', 'db')
- grad_key_weight: float32 [896, 4096], P(None, 'db')
- grad_value_weight: float32 [896, 4096], P(None, 'db')
- grad_kernel: float32 [3, 896], replicated
Inputs may be any that keep to these rules, and one draw needn't show every extreme that they name: `nbr_owner`: in the 9 spans of one index of dp no owner is named more than 2 times, a bound that some block reaches; the 2 neighbours of a span have different owners.
All inputs are finite; a program needn't handle non-finite values.
Results may differ from a plain program's by a relative error of at most 0.035.
The roundings to bfloat16 on the way count: a program that leaves them out, or rounds other values in their place, can miss the bound.
Values may be sent and summed in bfloat16 or wider, within the bound.
A program may use at most 192 MiB of HBM per device.

v0:
```python
import math
import jax
import jax.numpy as jnp
from jax import lax
from jax.sharding import PartitionSpec as P

HD = 128
ENC = 896
SPAN = 64
NBR = 2
NLEN = 128
KW = 3


def extended(block, sides, width):
    for axis, dim in sides:
        count = lax.axis_size(axis)
        forward = [(i, i + 1) for i in range(count - 1)]
        backward = [(target, source) for source, target in forward]
        low = lax.ppermute(
            lax.slice_in_dim(block, block.shape[dim] - width, None, axis=dim), axis, forward
        )
        high = lax.ppermute(lax.slice_in_dim(block, 0, width, axis=dim), axis, backward)
        block = jnp.concatenate([low, block, high], axis=dim)
    return block


def conv_apply(padded, kernel, length):
    summed = kernel[0] * padded[:, 0:length, :].astype(jnp.float32)
    for offset in range(1, KW):
        summed = summed + kernel[offset] * padded[:, offset : offset + length, :].astype(
            jnp.float32
        )
    return summed


def conv_adjoint(grad_padded, kernel, length):
    final_tap = KW - 1
    summed = kernel[0] * grad_padded[:, final_tap : final_tap + length, :]
    for offset in range(1, KW):
        begin = final_tap - offset
        summed = summed + kernel[offset] * grad_padded[:, begin : begin + length, :]
    return summed


def taps_gradient(grad_mixed, padded, length):
    return jnp.stack(
        [
            jnp.sum(
                grad_mixed * padded[:, offset : offset + length, :].astype(jnp.float32), axis=(0, 1)
            )
            for offset in range(KW)
        ]
    )


def shards(
    queries, cotangent, db_states, key_weight, value_weight, conv_kernel, nbr_owner, nbr_row
):
    half_taps = (KW - 1) // 2
    score_scale = 1.0 / math.sqrt(HD)
    owners = lax.axis_size("dp")
    span_count = nbr_owner.shape[0]
    request_count = span_count * NBR
    capacity = max(2, (request_count + owners - 1) // owners)
    quarter = db_states.shape[1]
    local_blocks = db_states.shape[0]
    slots_total = owners * capacity
    local_width = key_weight.shape[1]
    local_heads = local_width // HD
    owner_flat = nbr_owner.reshape(request_count)
    row_flat = nbr_row.reshape(request_count)
    positions = jnp.arange(request_count, dtype=jnp.int32)
    same_owner = owner_flat[:, None] == owner_flat[None, :]
    earlier = positions[:, None] > positions[None, :]
    slot_index = jnp.sum(jnp.logical_and(same_owner, earlier).astype(jnp.int32), axis=1)
    target = owner_flat * capacity + slot_index
    slot_hits = target[:, None] == jnp.arange(slots_total, dtype=jnp.int32)[None, :]
    used_slot = jnp.any(slot_hits, axis=0)
    row_sent = jnp.sum(jnp.where(slot_hits, row_flat[:, None], 0), axis=0)
    row_table = jnp.where(used_slot, row_sent, -1).reshape(owners, capacity)
    slot_matrix = slot_hits.astype(jnp.bfloat16)
    states_flat = db_states.reshape(local_blocks, quarter * ENC)
    asked = lax.all_to_all(row_table, "dp", split_axis=0, concat_axis=0, tiled=True)
    sources = asked.shape[0]
    items = asked.shape[1]
    asked_flat = asked.reshape(sources * items)
    picker = (asked_flat[:, None] == jnp.arange(local_blocks, dtype=jnp.int32)[None, :]).astype(
        jnp.bfloat16
    )
    fetched = jnp.dot(picker, states_flat, preferred_element_type=jnp.float32).astype(jnp.bfloat16)
    fetched = fetched.reshape(sources, items, quarter, ENC)
    replied = lax.all_to_all(fetched, "dp", split_axis=0, concat_axis=0, tiled=True)
    received = jnp.dot(
        slot_matrix, replied.reshape(slots_total, quarter * ENC), preferred_element_type=jnp.float32
    )
    received = received.astype(jnp.bfloat16).reshape(request_count, quarter, ENC)
    padded_part = extended(received, (("db", 1),), half_taps)
    mixed_part = conv_apply(padded_part, conv_kernel, quarter).astype(jnp.bfloat16)
    mixed = lax.all_gather(mixed_part, "db", axis=1, tiled=True)
    mixed_flat = mixed.reshape(request_count * NLEN, ENC)
    keys = jnp.dot(mixed_flat, key_weight, preferred_element_type=jnp.float32).astype(jnp.bfloat16)
    values = jnp.dot(mixed_flat, value_weight, preferred_element_type=jnp.float32).astype(
        jnp.bfloat16
    )
    key_heads = keys.reshape(span_count, NBR * NLEN, local_heads, HD)
    value_heads = values.reshape(span_count, NBR * NLEN, local_heads, HD)
    query_heads = queries.reshape(span_count, SPAN, local_heads, HD)
    grad_heads = cotangent.reshape(span_count, SPAN, local_heads, HD)
    scores = (
        jnp.einsum("cqhd,ckhd->chqk", query_heads, key_heads, preferred_element_type=jnp.float32)
        * score_scale
    )
    highest = jnp.max(scores, axis=-1, keepdims=True)
    expo = jnp.exp(scores - highest)
    probs = expo / jnp.sum(expo, axis=-1, keepdims=True)
    probs_b = probs.astype(jnp.bfloat16)
    attended = jnp.einsum(
        "chqk,ckhd->cqhd", probs_b, value_heads, preferred_element_type=jnp.float32
    ).astype(jnp.bfloat16)
    grad_probs = jnp.einsum(
        "cqhd,ckhd->chqk", grad_heads, value_heads, preferred_element_type=jnp.float32
    )
    grad_values = jnp.einsum(
        "chqk,cqhd->ckhd", probs_b, grad_heads, preferred_element_type=jnp.float32
    ).astype(jnp.bfloat16)
    inner = jnp.sum(grad_probs * probs, axis=-1, keepdims=True)
    grad_scores = (score_scale * probs * (grad_probs - inner)).astype(jnp.bfloat16)
    grad_query = jnp.einsum(
        "chqk,ckhd->cqhd", grad_scores, key_heads, preferred_element_type=jnp.float32
    ).astype(jnp.bfloat16)
    grad_keys = jnp.einsum(
        "chqk,cqhd->ckhd", grad_scores, query_heads, preferred_element_type=jnp.float32
    ).astype(jnp.bfloat16)
    keys_flat = grad_keys.reshape(request_count * NLEN, local_width)
    values_flat = grad_values.reshape(request_count * NLEN, local_width)
    key_term = jnp.einsum("ne,nf->ef", mixed_flat, keys_flat, preferred_element_type=jnp.float32)
    value_term = jnp.einsum(
        "ne,nf->ef", mixed_flat, values_flat, preferred_element_type=jnp.float32
    )
    grad_mixed = jnp.einsum("nf,ef->ne", keys_flat, key_weight, preferred_element_type=jnp.float32)
    grad_mixed = grad_mixed + jnp.einsum(
        "nf,ef->ne", values_flat, value_weight, preferred_element_type=jnp.float32
    )
    grad_mixed = grad_mixed.reshape(request_count, NLEN, ENC)
    grad_mixed_part = lax.psum_scatter(grad_mixed, "db", scatter_dimension=1, tiled=True)
    grad_padded = extended(grad_mixed_part, (("db", 1),), half_taps)
    grad_raw = conv_adjoint(grad_padded, conv_kernel, quarter)
    taps_term = taps_gradient(grad_mixed_part, padded_part, quarter)
    grad_raw_b = grad_raw.astype(jnp.bfloat16).reshape(request_count, quarter * ENC)
    grad_send = jnp.einsum(
        "ns,nf->sf", slot_matrix, grad_raw_b, preferred_element_type=jnp.float32
    ).astype(jnp.bfloat16)
    grad_send = grad_send.reshape(owners, capacity, quarter, ENC)
    grad_back = lax.all_to_all(grad_send, "dp", split_axis=0, concat_axis=0, tiled=True)
    asked_flat = asked.reshape(slots_total)
    picker_back = (
        jnp.arange(local_blocks, dtype=jnp.int32)[:, None] == asked_flat[None, :]
    ).astype(jnp.bfloat16)
    grad_states = jnp.dot(
        picker_back,
        grad_back.reshape(slots_total, quarter * ENC),
        preferred_element_type=jnp.float32,
    )
    grad_states = grad_states.reshape(local_blocks, quarter, ENC)
    grad_key_weight, grad_value_weight = lax.psum((key_term, value_term), "dp")
    grad_kernel = lax.psum(taps_term, ("dp", "db"))
    return (
        attended.reshape(span_count * SPAN, local_width),
        grad_query.reshape(span_count * SPAN, local_width),
        grad_states,
        grad_key_weight,
        grad_value_weight,
        grad_kernel,
    )


def solution(mesh):
    return jax.shard_map(
        shards,
        mesh=mesh,
        in_specs=(
            P("dp", "db"),
            P("dp", "db"),
            P("dp", "db", None),
            P(None, "db"),
            P(None, "db"),
            P(),
            P("dp", None),
            P("dp", None),
        ),
        out_specs=(
            P("dp", "db"),
            P("dp", "db"),
            P("dp", "db", None),
            P(None, "db"),
            P(None, "db"),
            P(),
        ),
        check_vma=False,
    )
```

profile of v0, /device:TPU:6, one launch (start us, length us, event | category | flops | bytes accessed | tf_op | source)
XLA Modules:
  0.0 488.2 jit_solution(10462257573725515154)
XLA Ops:
  10.1 8.4 %all-to-all-start = ((s32[32,1,2]{2,1,0:T(1,128)}), s32[32,1,2]{2,1,0:T(1,128)S(1)}, u32[]{:S(2)}, u32[]{:S(2)}) async-start(s32[32,1,2]{2,1,0:T(1,128)} %bitcast), calls=%async_computation | async-start | bytes 32768 | tf_op jit(solution)/shard_map/all_to_all | solution.py:84
  18.6 3.3 copy.76
  21.9 2.1 all-to-all-done
  25.3 2.6 convolution_convert_fusion.1
  28.5 48.2 %all_to_all.16 = bf16[32,2,32,896]{3,2,1,0:T(8,128)(2,1)S(1)} all-to-all(bf16[32,2,32,896]{3,2,1,0:T(8,128)(2,1)S(1)} %bitcast.131), channel_id=1, replica_groups=mesh['dp'=32,'db'=4] {'dp'}, dimensions={0} | all-to-all | bytes 7340032 | tf_op jit(solution)/shard_map/all_to_all | solution.py:93
  76.8 1.4 copy.78
  79.1 3.5 collective-permute-start
  82.6 1.3 collective-permute-start.1
  85.0 4.3 collective-permute-done.1
  89.2 1.8 fusion.36
  91.3 1.6 copy.81
  92.9 2.6 copy.84
  95.5 42.6 %all-gather.2.cloned.1.call-done = bf16[18,128,896]{2,1,0:T(8,128)(2,1)} async-done(((bf16[18,32,896]{2,1,0:T(8,128)(2,1)}), bf16[18,128,896]{2,1,0:T(8,128)(2,1)}) %all-gather.2.cloned.1.call-update) | async-done | bytes 4128784 | tf_op jit(solution)/shard_map/all_gather | solution.py:100
  138.1 7.4 %fusion.33 = bf16[288,8,8,128]{3,1,2,0:T(8,128)(2,1)S(1)} fusion(bf16[2304,896]{1,0:T(8,128)(2,1)} %bitcast.159, bf16[896,1024]{1,0:T(8,128)(2,1)S(1)} %copy-done), kind=kOutput, calls=%fused_computation.50 | convolution fusion | flops 4230217728 | bytes 10682368 | tf_op jit(solution)/shard_map/dot_general | solution.py:102
  145.6 1.3 copy.80
  148.3 5.5 %fusion.32 = bf16[288,8,8,128]{3,1,2,0:T(8,128)(2,1)S(1)} fusion(bf16[2304,896]{1,0:T(8,128)(2,1)S(1)} %bitcast.162, bf16[896,1024]{1,0:T(8,128)(2,1)S(1)} %copy-done.17), kind=kOutput, calls=%fused_computation.49 | convolution fusion | flops 4230217728 | bytes 10682368 | tf_op jit(solution)/shard_map/dot_general | solution.py:103
  153.8 3.4 copy.82
  157.2 1.8 fusion.23
  158.9 3.6 fusion.82
  162.5 15.7 %convert_bitcast_fusion = bf16[9,256,8,128]{3,1,2,0:T(8,128)(2,1)} fusion(bf16[9,64,8,128]{3,2,1,0:T(8,128)(2,1)} %bitcast.157, f32[9,8,64]{2,1,0:T(8,128)S(1)} %get-tuple-element.43, f32[9,8,256,64]{2,3,1,0:T(8,128)} %copy-done.5), kind=kOutput, calls=%fused_computation.23 | convolution fusion | flops 310252288 | bytes 10635264 | tf_op jit(solution)/shard_map/chqk,cqhd->ckhd/dot_general | solution.py:124
  178.2 5.7 %copy.72 = bf16[9,256,8,128]{3,2,1,0:T(8,128)(2,1)S(1)} copy(bf16[9,256,8,128]{3,1,2,0:T(8,128)(2,1)} %convert_bitcast_fusion) | data formatting | bytes 9437184 | tf_op jit(solution)/shard_map/convert_element_type | solution.py:126
  184.0 5.8 %fusion.8 = (f32[9,8,64]{2,1,0:T(8,128)S(1)}, f32[9,8,256,64]{2,3,1,0:T(8,128)S(1)}) fusion(f32[9,8,64,256]{3,2,1,0:T(8,128)S(1)} %copy-done.4, f32[9,8,64]{2,1,0:T(8,128)S(1)} %get-tuple-element.43, bf16[9,64,8,128]{3,2,1,0:T(8,128)(2,1)S(1)} %bitcast.158, bf16[9,256,8,128]{3,2,1,0:T(8,128)(2,1)} %bitcast.146), kind=kOutput, calls=%fused_computation.16 | convolution fusion | flops 305524224 | bytes 15372288 | tf_op jit(solution)/shard_map/cqhd,ckhd->chqk/dot_general | solution.py:121
  189.8 1.5 fusion.10
  191.3 1.4 copy-done.3
  192.7 1.7 convert_bitcast_fusion.1
  194.4 3.3 copy.70
  197.7 7.3 %fusion.6 = f32[2304,896]{1,0:T(8,128)} fusion(bf16[896,1024]{1,0:T(8,128)(2,1)S(1)} %copy-done, bf16[288,8,8,128]{3,2,1,0:T(8,128)(2,1)S(1)} %bitcast.150), kind=kOutput, calls=%fused_computation.12 | convolution fusion | flops 4227858432 | bytes 14811136 | tf_op jit(solution)/shard_map/nf,ef->ne/dot_general | solution.py:141
  205.0 9.5 %convolution_add_fusion = f32[2304,896]{1,0:T(8,128)} fusion(f32[2304,896]{1,0:T(8,128)} %fusion.6, bf16[896,1024]{1,0:T(8,128)(2,1)S(1)} %copy-done.18, bf16[288,8,8,128]{3,2,1,0:T(8,128)(2,1)S(1)} %bitcast.148), kind=kOutput, calls=%fused_computation.4 | convolution fusion | flops 4229922816 | bytes 23068672 | tf_op jit(solution)/shard_map/nf,ef->ne/dot_general | solution.py:142
  214.4 79.9 %reduce-scatter.2.cloned.1.call-done = f32[18,32,896]{2,1,0:T(8,128)} async-done(((f32[18,128,896]{2,1,0:T(8,128)}), f32[18,32,896]{2,1,0:T(8,128)}) %reduce-scatter.2.cloned.1.call-update) | async-done | bytes 2064400 | tf_op jit(solution)/shard_map/reduce_scatter | solution.py:146
  294.4 1.3 fusion.80
  295.6 1.3 collective-permute-start.2
  297.0 5.3 %collective-permute-start.3 = (f32[18,1,896]{2,1,0:T(1,128)S(1)}, f32[18,1,896]{2,1,0:T(1,128)S(1)}, u32[]{:S(2)}, u32[]{:S(2)}) collective-permute-start(f32[18,1,896]{2,1,0:T(1,128)S(1)} %get-tuple-element.40), channel_id=1, source_target_pairs={{0,1},{1,2},{2,3},{4,5},{5,6},{6,7},{8,9},{9,10},{10,11},{12,13},{... | collective-permute-start | bytes 193544 | tf_op jit(solution)/shard_map/ppermute | solution.py:20
  302.3 9.9 %fusion.4 = f32[896,1024]{1,0:T(8,128)} fusion(bf16[2304,896]{1,0:T(8,128)(2,1)} %bitcast.160, bf16[288,8,8,128]{3,2,1,0:T(8,128)(2,1)} %bitcast.151), kind=kOutput, calls=%fused_computation.10 | convolution fusion | flops 4227858432 | bytes 12517376 | tf_op jit(solution)/shard_map/ne,nf->ef/dot_general | solution.py:137
  312.2 2.2 fusion.37
  315.0 1.2 convolution_convert_fusion
  316.2 2.4 copy.89
  318.6 7.6 %all-to-all-start.2 = ((bf16[32,2,32,896]{3,2,1,0:T(8,128)(2,1)}), bf16[32,2,32,896]{3,2,1,0:T(8,128)(2,1)}, u32[]{:S(2)}, u32[]{:S(2)}) async-start(bf16[32,2,32,896]{3,2,1,0:T(8,128)(2,1)} %bitcast.130), calls=%async_computation.3 | async-start | bytes 7340032 | tf_op jit(solution)/shard_map/all_to_all | solution.py:155
  326.5 9.9 %fusion.1 = f32[896,1024]{1,0:T(8,128)} fusion(bf16[2304,896]{1,0:T(8,128)(2,1)} %bitcast.161, bf16[288,8,8,128]{3,2,1,0:T(8,128)(2,1)} %bitcast.149), kind=kOutput, calls=%fused_computation.7 | convolution fusion | flops 4227858432 | bytes 12517376 | tf_op jit(solution)/shard_map/ne,nf->ef/dot_general | solution.py:138
  336.4 3.8 fusion.54
  341.1 14.0 %fusion.51 = bf16[9,64,8,128]{3,1,2,0:T(8,128)(2,1)S(1)} fusion(bf16[9,256,8,128]{3,2,1,0:T(8,128)(2,1)} %bitcast.147, f32[9,8,64]{2,1,0:T(8,128)S(1)} %get-tuple-element.43, f32[9,8,256,64]{2,3,1,0:T(8,128)} %copy-done.5), kind=kOutput, calls=%fused_computation.66 | convolution fusion | flops 308482816 | bytes 10635264 | tf_op jit(solution)/shard_map/chqk,ckhd->cqhd/dot_general | solution.py:118
  355.0 1.0 copy.64
  356.1 2.0 copy_bitcast_fusion
  358.1 73.3 %psum.23 = f32[3,896]{1,0:T(4,128)} all-reduce(f32[3,896]{1,0:T(4,128)S(1)} %pad_maximum_fusion.4), channel_id=1, replica_groups=mesh['dp'=32,'db'=4] {'dp','db'}, use_global_device_ids=true, to_apply=%region_12.13 | all-reduce | flops 2688 | bytes 21504 | tf_op jit(solution)/shard_map/psum | solution.py:167
  431.4 4.4 fusion.26
  435.8 4.0 copy.74
  439.8 35.3 %all-reduce.3.cloned.1.call-done = (f32[896,1024]{1,0:T(8,128)}, f32[896,1024]{1,0:T(8,128)}) async-done(((f32[896,1024]{1,0:T(8,128)}, f32[896,1024]{1,0:T(8,128)}), (f32[896,1024]{1,0:T(8,128)}, f32[896,1024]{1,0:T(8,128)})) %all-reduce.3.cloned.1.call-update) | async-done | bytes 7340048 | tf_op jit(solution)/shard_map/psum | solution.py:166
  475.1 4.5 copy.146
  479.6 1.8 copy.147
  (73 shorter events, 10.2 us)
Async XLA Ops:
  7.2 131.0 %copy-start = (bf16[896,1024]{1,0:T(8,128)(2,1)S(1)}, bf16[896,1024]{1,0:T(8,128)(2,1)}, u32[]{:S(2)}) copy-start(bf16[896,1024]{1,0:T(8,128)(2,1)} %param.11) | copy-start | bytes 5505028
  10.1 13.9 %all-to-all-start = ((s32[32,1,2]{2,1,0:T(1,128)}), s32[32,1,2]{2,1,0:T(1,128)S(1)}, u32[]{:S(2)}, u32[]{:S(2)}) async-start(s32[32,1,2]{2,1,0:T(1,128)} %bitcast), calls=%async_computation | async-start | bytes 32768 | tf_op jit(solution)/shard_map/all_to_all | solution.py:84
  18.5 119.6 %all-gather.2.cloned.1.call-start = ((), (), s32[]{:S(2)}) async-start(), calls=%async_computation.4 | async-start | bytes 5160960 | tf_op jit(solution)/shard_map/all_gather | solution.py:100
  78.1 5.8 %copy-start.15 = (f32[3,896]{1,0:T(4,128)S(1)}, f32[3,896]{1,0:T(4,128)}, u32[]{:S(2)}) copy-start(f32[3,896]{1,0:T(4,128)} %param.13) | copy-start | bytes 32260
  79.0 5.0 %copy-start.8 = (bf16[3,8,32,896]{3,2,1,0:T(8,128)(2,1)}, bf16[3,8,32,896]{3,2,1,0:T(8,128)(2,1)S(1)}, u32[]{:S(2)}) copy-start(bf16[3,8,32,896]{3,2,1,0:T(8,128)(2,1)S(1)} %copy.79) | copy-start | bytes 4128772
  79.1 5.9 %collective-permute-start = (bf16[18,1,896]{2,1,0:T(2,128)(2,1)S(1)}, bf16[18,1,896]{2,1,0:T(2,128)(2,1)S(1)}, u32[]{:S(2)}, u32[]{:S(2)}) collective-permute-start(bf16[18,1,896]{2,1,0:T(2,128)(2,1)S(1)} %get-tuple-element.41), channel_id=1, source_target_pairs={{0,1},{1,2},{2,3},{4,5},{5,6},{6,7},{8,9},{9,10},{10,11},{12,13},{... | collective-permute-start | bytes 96776 | tf_op jit(solution)/shard_map/ppermute | solution.py:20
  82.6 6.6 %collective-permute-start.1 = (bf16[18,1,896]{2,1,0:T(2,128)(2,1)S(1)}, bf16[18,1,896]{2,1,0:T(2,128)(2,1)S(1)}, u32[]{:S(2)}, u32[]{:S(2)}) collective-permute-start(bf16[18,1,896]{2,1,0:T(2,128)(2,1)S(1)} %get-tuple-element.42), channel_id=1, source_target_pairs={{1,0},{2,1},{3,2},{5,4},{6,5},{7,6},{9,8},{10,9},{11,10},{13,12},{... | collective-permute-start | bytes 96776 | tf_op jit(solution)/shard_map/ppermute | solution.py:23
  84.1 5.2 %copy-start.6 = (bf16[18,32,896]{2,1,0:T(8,128)(2,1)}, bf16[18,32,896]{2,1,0:T(8,128)(2,1)S(1)}, u32[]{:S(2)}) copy-start(bf16[18,32,896]{2,1,0:T(8,128)(2,1)S(1)} %slice.57) | copy-start | bytes 3096580
  91.1 203.2 %reduce-scatter.2.cloned.1.call-start = ((), (), s32[]{:S(2)}) async-start(), calls=%async_computation.5 | async-start | bytes 10321920 | tf_op jit(solution)/shard_map/reduce_scatter | solution.py:146
  145.6 2.2 copy-start.16
  145.6 2.7 copy-start.17
  148.3 8.8 %copy-start.2 = (bf16[288,8,8,128]{3,2,1,0:T(8,128)(2,1)}, bf16[288,8,8,128]{3,2,1,0:T(8,128)(2,1)S(1)}, u32[]{:S(2)}) copy-start(bf16[288,8,8,128]{3,2,1,0:T(8,128)(2,1)S(1)} %copy.80) | copy-start | bytes 14155780
  158.9 3.6 copy-start.5
  178.2 5.8 %copy-start.4 = (f32[9,8,64,256]{3,2,1,0:T(8,128)S(1)}, f32[9,8,64,256]{3,2,1,0:T(8,128)}, u32[]{:S(2)}) copy-start(f32[9,8,64,256]{3,2,1,0:T(8,128)} %get-tuple-element.44) | copy-start | bytes 14155780
  178.2 5.8 %copy-start.14 = (bf16[72,8,8,128]{3,2,1,0:T(8,128)(2,1)S(1)}, bf16[72,8,8,128]{3,2,1,0:T(8,128)(2,1)}, u32[]{:S(2)}) copy-start(bf16[72,8,8,128]{3,2,1,0:T(8,128)(2,1)} %copy.84) | copy-start | bytes 3538948
  183.9 21.0 %copy-start.10 = (bf16[9,256,8,128]{3,2,1,0:T(8,128)(2,1)}, bf16[9,256,8,128]{3,2,1,0:T(8,128)(2,1)S(1)}, u32[]{:S(2)}) copy-start(bf16[9,256,8,128]{3,2,1,0:T(8,128)(2,1)S(1)} %copy.72) | copy-start | bytes 14155780
  191.3 1.4 copy-start.3
  197.7 7.3 %copy-start.11 = (bf16[9,256,8,128]{3,2,1,0:T(8,128)(2,1)}, bf16[9,256,8,128]{3,2,1,0:T(8,128)(2,1)S(1)}, u32[]{:S(2)}) copy-start(bf16[9,256,8,128]{3,2,1,0:T(8,128)(2,1)S(1)} %copy.70) | copy-start | bytes 14155780
  197.7 7.3 %copy-start.18 = (bf16[896,1024]{1,0:T(8,128)(2,1)S(1)}, bf16[896,1024]{1,0:T(8,128)(2,1)}, u32[]{:S(2)}) copy-start(bf16[896,1024]{1,0:T(8,128)(2,1)} %param.12) | copy-start | bytes 5505028
  295.6 16.5 %collective-permute-start.2 = (f32[18,1,896]{2,1,0:T(1,128)S(1)}, f32[18,1,896]{2,1,0:T(1,128)S(1)}, u32[]{:S(2)}, u32[]{:S(2)}) collective-permute-start(f32[18,1,896]{2,1,0:T(1,128)S(1)} %get-tuple-element.39), channel_id=1, source_target_pairs={{1,0},{2,1},{3,2},{5,4},{6,5},{7,6},{9,8},{10,9},{11,10},{13,12},{... | collective-permute-start | bytes 193544 | tf_op jit(solution)/shard_map/ppermute | solution.py:23
  296.9 15.2 %copy-start.7 = (bf16[18,32,896]{2,1,0:T(8,128)(2,1)S(1)}, bf16[18,32,896]{2,1,0:T(8,128)(2,1)}, u32[]{:S(2)}) copy-start(bf16[18,32,896]{2,1,0:T(8,128)(2,1)} %copy-done.6) | copy-start | bytes 3096580
  297.0 15.2 %copy-start.9 = (bf16[3,8,32,896]{3,2,1,0:T(8,128)(2,1)S(1)}, bf16[3,8,32,896]{3,2,1,0:T(8,128)(2,1)}, u32[]{:S(2)}) copy-start(bf16[3,8,32,896]{3,2,1,0:T(8,128)(2,1)} %copy-done.8) | copy-start | bytes 4128772
  297.0 15.2 %copy-start.13 = (f32[18,32,896]{2,1,0:T(8,128)S(1)}, f32[18,32,896]{2,1,0:T(8,128)}, u32[]{:S(2)}) copy-start(f32[18,32,896]{2,1,0:T(8,128)} %reduce-scatter.2.cloned.1.call-done) | copy-start | bytes 6193156
  297.0 15.2 %collective-permute-start.3 = (f32[18,1,896]{2,1,0:T(1,128)S(1)}, f32[18,1,896]{2,1,0:T(1,128)S(1)}, u32[]{:S(2)}, u32[]{:S(2)}) collective-permute-start(f32[18,1,896]{2,1,0:T(1,128)S(1)} %get-tuple-element.40), channel_id=1, source_target_pairs={{0,1},{1,2},{2,3},{4,5},{5,6},{6,7},{8,9},{9,10},{10,11},{12,13},{... | collective-permute-start | bytes 193544 | tf_op jit(solution)/shard_map/ppermute | solution.py:20
  318.6 112.8 %all-to-all-start.2 = ((bf16[32,2,32,896]{3,2,1,0:T(8,128)(2,1)}), bf16[32,2,32,896]{3,2,1,0:T(8,128)(2,1)}, u32[]{:S(2)}, u32[]{:S(2)}) async-start(bf16[32,2,32,896]{3,2,1,0:T(8,128)(2,1)} %bitcast.130), calls=%async_computation.3 | async-start | bytes 7340032 | tf_op jit(solution)/shard_map/all_to_all | solution.py:155
  326.2 148.8 %all-reduce.3.cloned.1.call-start = ((), (), s32[]{:S(2)}) async-start(), calls=%async_computation.6 | async-start | bytes 14680064 | tf_op jit(solution)/shard_map/psum | solution.py:166
  475.1 4.5 copy-start.12
  475.1 6.4 %copy-start.1 = (bf16[896,1024]{1,0:T(8,128)(2,1)S(1)}, bf16[896,1024]{1,0:T(8,128)(2,1)}, u32[]{:S(2)}) copy-start(bf16[896,1024]{1,0:T(8,128)(2,1)} %param.11) | copy-start | bytes 5505028
Sparse Core Ops, SparseCore 0:
  91.2 46.8 all-gather.1
  214.6 79.7 reduce-scatter.1
  336.5 138.5 all-reduce.2
where the time goes:
time: 494 us; the launch traced here: 488 us
  waiting for transfers between devices  165 us (33%)
  blocking collectives  122 us (25%)
  matrix products  101 us (20%)
  local copies, waits for them, and re-layouts  48.1 us (10%)
  starting transfers between devices  27.8 us (6%)
  between operations  14.4 us (3%)
  other arithmetic  10.2 us (2%)
    reduce_scatter x1, waiting for transfers between devices, shards(): lax.psum_scatter(grad_mixed, 'db', scatter_dimension=1, tiled=True)  79.9 us
    psum x1, blocking collectives, shards(): grad_kernel = lax.psum(taps_term, ('dp', 'db'))  73.3 us
    all_to_all x1, blocking collectives, shards(): lax.all_to_all(fetched, 'dp', split_axis=0, concat_axis=0, tiled=True)  48.2 us
    all_gather x1, waiting for transfers between devices, shards(): mixed = lax.all_gather(mixed_part, 'db', axis=1, tiled=True)  42.6 us
    psum x1, waiting for transfers between devices, shards(): grad_key_weight, grad_value_weight = lax.psum((key_term, value_term), 'dp')  35.3 us
    unnamed x54, local copies, waits for them, and re-layouts  32.2 us
    dot_general x1, matrix products, shards(): jnp.einsum('chqk,cqhd->ckhd', probs_b, grad_heads, preferred_element_type...  15.7 us
    dot_general x1, matrix products, shards(): jnp.einsum('chqk,ckhd->cqhd', probs_b, value_heads, preferred_element_typ...  14 us
  transfers between devices with their start and end apart: 9, of which 6 were waited for; matrix products, arithmetic and copies ran while one was open for 12% of the time, Pallas kernels for 0%

commit v1 on v0

--- a/solution.py
+++ b/solution.py
@@ -164,7 +164,8 @@
     )
     grad_states = grad_states.reshape(local_blocks, quarter, ENC)
     grad_key_weight, grad_value_weight = lax.psum((key_term, value_term), "dp")
-    grad_kernel = lax.psum(taps_term, ("dp", "db"))
+    pieces = lax.all_gather(taps_term, ("dp", "db"))
+    grad_kernel = jnp.sum(pieces, axis=0)
     return (
         attended.reshape(span_count * SPAN, local_width),
         grad_query.reshape(span_count * SPAN, local_width),

time: 494 us -> 538 us (1.089)
  waiting for transfers between devices: 165 us -> 276 us
  blocking collectives: 122 us -> 48.2 us
  other arithmetic: 10.2 us -> 17.4 us
    psum x1, waiting for transfers between devices: 35.3 us -> 112 us  [shards(): grad_key_weight, grad_value_weight = lax.psum((key_term, value_term), 'dp')]
    psum x1 -> x0, blocking collectives: 73.3 us -> none  [shards(): grad_kernel = lax.psum(taps_term, ('dp', 'db'))]
    all_gather x0 -> x1, waiting for transfers between devices: none -> 33 us  [shards(): pieces = lax.all_gather(taps_term, ('dp', 'db'))]
  transfers between devices with their start and end apart: 9 -> 10, of which waited for: 6 -> 9; matrix products, arithmetic and copies ran while one was open for 12% -> 12% of each run, Pallas kernels for 0% -> 0%
where the time goes in v1:
time: 538 us; the launch traced here: 532 us
  waiting for transfers between devices  276 us (51%)
  matrix products  100 us (19%)
  blocking collectives  48.2 us (9%)
  local copies, waits for them, and re-layouts  48.1 us (9%)
  starting transfers between devices  27.1 us (5%)
  other arithmetic  17.4 us (3%)
  between operations  14.4 us (3%)
    psum x1, waiting for transfers between devices, shards(): grad_key_weight, grad_value_weight = lax.psum((key_term, value_term), 'dp')  112 us
    reduce_scatter x1, waiting for transfers between devices, shards(): lax.psum_scatter(grad_mixed, 'db', scatter_dimension=1, tiled=True)  79.9 us
    all_to_all x1, blocking collectives, shards(): lax.all_to_all(fetched, 'dp', split_axis=0, concat_axis=0, tiled=True)  48.2 us
    all_gather x1, waiting for transfers between devices, shards(): mixed = lax.all_gather(mixed_part, 'db', axis=1, tiled=True)  42.6 us
    all_gather x1, waiting for transfers between devices, shards(): pieces = lax.all_gather(taps_term, ('dp', 'db'))  33 us
    unnamed x54, local copies, waits for them, and re-layouts  32.2 us
    dot_general x1, matrix products, shards(): jnp.einsum('chqk,cqhd->ckhd', probs_b, grad_heads, preferred_element_type...  15.7 us
    dot_general x1, matrix products, shards(): jnp.einsum('chqk,ckhd->cqhd', probs_b, value_heads, preferred_element_typ...  13.3 us
  transfers between devices with their start and end apart: 10, of which 9 were waited for; matrix products, arithmetic and copies ran while one was open for 12% of the time, Pallas kernels for 0%

profile of v1, /device:TPU:6, one launch (start us, length us, event | category | flops | bytes accessed | tf_op | source)
XLA Modules:
  0.0 532.0 jit_solution(7261440808703379059)
XLA Ops:
  10.1 8.4 %all-to-all-start = ((s32[32,1,2]{2,1,0:T(1,128)}), s32[32,1,2]{2,1,0:T(1,128)S(1)}, u32[]{:S(2)}, u32[]{:S(2)}) async-start(s32[32,1,2]{2,1,0:T(1,128)} %bitcast), calls=%async_computation | async-start | bytes 32768 | tf_op jit(solution)/shard_map/all_to_all | solution.py:84
  18.6 3.3 copy.76
  21.9 2.1 all-to-all-done
  25.3 2.6 convolution_convert_fusion.1
  28.5 48.2 %all_to_all.16 = bf16[32,2,32,896]{3,2,1,0:T(8,128)(2,1)S(1)} all-to-all(bf16[32,2,32,896]{3,2,1,0:T(8,128)(2,1)S(1)} %bitcast.133), channel_id=1, replica_groups=mesh['dp'=32,'db'=4] {'dp'}, dimensions={0} | all-to-all | bytes 7340032 | tf_op jit(solution)/shard_map/all_to_all | solution.py:93
  76.8 1.4 copy.78
  79.1 3.5 collective-permute-start
  82.6 1.3 collective-permute-start.1
  85.0 4.3 collective-permute-done.1
  89.2 1.8 fusion.36
  91.3 1.6 copy.81
  92.9 2.6 copy.84
  95.5 42.6 %all-gather.5.cloned.1.call-done = bf16[18,128,896]{2,1,0:T(8,128)(2,1)} async-done(((bf16[18,32,896]{2,1,0:T(8,128)(2,1)}), bf16[18,128,896]{2,1,0:T(8,128)(2,1)}) %all-gather.5.cloned.1.call-update) | async-done | bytes 4128784 | tf_op jit(solution)/shard_map/all_gather | solution.py:100
  138.1 7.4 %fusion.33 = bf16[288,8,8,128]{3,1,2,0:T(8,128)(2,1)S(1)} fusion(bf16[2304,896]{1,0:T(8,128)(2,1)} %bitcast.161, bf16[896,1024]{1,0:T(8,128)(2,1)S(1)} %copy-done), kind=kOutput, calls=%fused_computation.50 | convolution fusion | flops 4230217728 | bytes 10682368 | tf_op jit(solution)/shard_map/dot_general | solution.py:102
  145.6 1.3 copy.80
  148.3 5.5 %fusion.32 = bf16[288,8,8,128]{3,1,2,0:T(8,128)(2,1)S(1)} fusion(bf16[2304,896]{1,0:T(8,128)(2,1)S(1)} %bitcast.164, bf16[896,1024]{1,0:T(8,128)(2,1)S(1)} %copy-done.17), kind=kOutput, calls=%fused_computation.49 | convolution fusion | flops 4230217728 | bytes 10682368 | tf_op jit(solution)/shard_map/dot_general | solution.py:103
  153.8 3.4 copy.82
  157.2 1.8 fusion.23
  158.9 3.6 fusion.82
  162.5 15.7 %convert_bitcast_fusion = bf16[9,256,8,128]{3,1,2,0:T(8,128)(2,1)} fusion(bf16[9,64,8,128]{3,2,1,0:T(8,128)(2,1)} %bitcast.159, f32[9,8,64]{2,1,0:T(8,128)S(1)} %get-tuple-element.43, f32[9,8,256,64]{2,3,1,0:T(8,128)} %copy-done.5), kind=kOutput, calls=%fused_computation.23 | convolution fusion | flops 310252288 | bytes 10635264 | tf_op jit(solution)/shard_map/chqk,cqhd->ckhd/dot_general | solution.py:124
  178.2 5.7 %copy.72 = bf16[9,256,8,128]{3,2,1,0:T(8,128)(2,1)S(1)} copy(bf16[9,256,8,128]{3,1,2,0:T(8,128)(2,1)} %convert_bitcast_fusion) | data formatting | bytes 9437184 | tf_op jit(solution)/shard_map/convert_element_type | solution.py:126
  184.0 5.8 %fusion.8 = (f32[9,8,64]{2,1,0:T(8,128)S(1)}, f32[9,8,256,64]{2,3,1,0:T(8,128)S(1)}) fusion(f32[9,8,64,256]{3,2,1,0:T(8,128)S(1)} %copy-done.4, f32[9,8,64]{2,1,0:T(8,128)S(1)} %get-tuple-element.43, bf16[9,64,8,128]{3,2,1,0:T(8,128)(2,1)S(1)} %bitcast.160, bf16[9,256,8,128]{3,2,1,0:T(8,128)(2,1)} %bitcast.148), kind=kOutput, calls=%fused_computation.16 | convolution fusion | flops 305524224 | bytes 15372288 | tf_op jit(solution)/shard_map/cqhd,ckhd->chqk/dot_general | solution.py:121
  189.8 1.5 fusion.10
  191.3 1.4 copy-done.3
  192.7 1.7 convert_bitcast_fusion.1
  194.4 3.3 copy.70
  197.7 7.3 %fusion.6 = f32[2304,896]{1,0:T(8,128)} fusion(bf16[896,1024]{1,0:T(8,128)(2,1)S(1)} %copy-done, bf16[288,8,8,128]{3,2,1,0:T(8,128)(2,1)S(1)} %bitcast.152), kind=kOutput, calls=%fused_computation.12 | convolution fusion | flops 4227858432 | bytes 14811136 | tf_op jit(solution)/shard_map/nf,ef->ne/dot_general | solution.py:141
  205.0 9.5 %convolution_add_fusion = f32[2304,896]{1,0:T(8,128)} fusion(f32[2304,896]{1,0:T(8,128)} %fusion.6, bf16[896,1024]{1,0:T(8,128)(2,1)S(1)} %copy-done.18, bf16[288,8,8,128]{3,2,1,0:T(8,128)(2,1)S(1)} %bitcast.150), kind=kOutput, calls=%fused_computation.4 | convolution fusion | flops 4229922816 | bytes 23068672 | tf_op jit(solution)/shard_map/nf,ef->ne/dot_general | solution.py:142
  214.5 79.9 %reduce-scatter.2.cloned.1.call-done = f32[18,32,896]{2,1,0:T(8,128)} async-done(((f32[18,128,896]{2,1,0:T(8,128)}), f32[18,32,896]{2,1,0:T(8,128)}) %reduce-scatter.2.cloned.1.call-update) | async-done | bytes 2064400 | tf_op jit(solution)/shard_map/reduce_scatter | solution.py:146
  294.3 1.3 fusion.80
  295.6 1.3 collective-permute-start.2
  296.9 4.5 collective-permute-start.3
  301.8 1.6 collective-permute-done.3
  303.4 6.4 %fusion.37 = (f32[896]{0:T(1024)S(1)}, f32[896]{0:T(1024)S(1)}, f32[896]{0:T(1024)S(1)}, bf16[18,32,896]{2,1,0:T(8,128)(2,1)}) fusion(f32[18,32,896]{2,1,0:T(8,128)} %reduce-scatter.2.cloned.1.call-done, bf16[18,32,896]{2,1,0:T(8,128)(2,1)S(1)} %copy-done.7, bf16[18,1,896]{2,1,0:T(2,128)(2,1)S(1)} %collective-permute-done, ...), kind=kLoop, calls=%fused_computation.54 | loop fusion | flops 11867520 | bytes 5376000 | tf_op jit(solution)/shard_map/reduce_sum | solution.py:49
  310.4 10.0 %fusion.4 = f32[896,1024]{1,0:T(8,128)} fusion(bf16[2304,896]{1,0:T(8,128)(2,1)} %bitcast.162, bf16[288,8,8,128]{3,2,1,0:T(8,128)(2,1)} %bitcast.153), kind=kOutput, calls=%fused_computation.10 | convolution fusion | flops 4227858432 | bytes 12517376 | tf_op jit(solution)/shard_map/ne,nf->ef/dot_general | solution.py:137
  322.2 2.4 copy.89
  324.6 7.6 %all-to-all-start.2 = ((bf16[32,2,32,896]{3,2,1,0:T(8,128)(2,1)}), bf16[32,2,32,896]{3,2,1,0:T(8,128)(2,1)}, u32[]{:S(2)}, u32[]{:S(2)}) async-start(bf16[32,2,32,896]{3,2,1,0:T(8,128)(2,1)} %bitcast.132), calls=%async_computation.3 | async-start | bytes 7340032 | tf_op jit(solution)/shard_map/all_to_all | solution.py:155
  332.4 9.9 %fusion.1 = f32[896,1024]{1,0:T(8,128)} fusion(bf16[2304,896]{1,0:T(8,128)(2,1)} %bitcast.163, bf16[288,8,8,128]{3,2,1,0:T(8,128)(2,1)} %bitcast.151), kind=kOutput, calls=%fused_computation.7 | convolution fusion | flops 4227858432 | bytes 12517376 | tf_op jit(solution)/shard_map/ne,nf->ef/dot_general | solution.py:138
  342.3 3.8 fusion.54
  347.0 13.3 %fusion.51 = bf16[9,64,8,128]{3,1,2,0:T(8,128)(2,1)S(1)} fusion(bf16[9,256,8,128]{3,2,1,0:T(8,128)(2,1)} %bitcast.149, f32[9,8,64]{2,1,0:T(8,128)S(1)} %get-tuple-element.43, f32[9,8,256,64]{2,3,1,0:T(8,128)} %copy-done.5), kind=kOutput, calls=%fused_computation.66 | convolution fusion | flops 308482816 | bytes 10635264 | tf_op jit(solution)/shard_map/chqk,ckhd->cqhd/dot_general | solution.py:118
  361.3 2.0 copy_bitcast_fusion
  363.3 33.0 %all-gather.7.cloned.1.call-done = f32[128,3,896]{2,1,0:T(4,128)} async-done(((f32[1,3,896]{2,1,0:T(4,128)}), f32[128,3,896]{2,1,0:T(4,128)}) %all-gather.7.cloned.1.call-update) | async-done | bytes 1376272 | tf_op jit(solution)/shard_map/all_gather | solution.py:167
  396.3 2.4 reduce_sum.79
  398.7 4.3 fusion.26
  403.1 4.0 copy.74
  407.0 111.9 %all-reduce.3.cloned.1.call-done = (f32[896,1024]{1,0:T(8,128)}, f32[896,1024]{1,0:T(8,128)}) async-done(((f32[896,1024]{1,0:T(8,128)}, f32[896,1024]{1,0:T(8,128)}), (f32[896,1024]{1,0:T(8,128)}, f32[896,1024]{1,0:T(8,128)})) %all-reduce.3.cloned.1.call-update) | async-done | bytes 7340048 | tf_op jit(solution)/shard_map/psum | solution.py:166
  518.9 4.5 copy.146
  523.4 1.8 copy.147
  (76 shorter events, 13.4 us)
Async XLA Ops:
  7.2 131.0 %copy-start = (bf16[896,1024]{1,0:T(8,128)(2,1)S(1)}, bf16[896,1024]{1,0:T(8,128)(2,1)}, u32[]{:S(2)}) copy-start(bf16[896,1024]{1,0:T(8,128)(2,1)} %param.11) | copy-start | bytes 5505028
  10.1 13.9 %all-to-all-start = ((s32[32,1,2]{2,1,0:T(1,128)}), s32[32,1,2]{2,1,0:T(1,128)S(1)}, u32[]{:S(2)}, u32[]{:S(2)}) async-start(s32[32,1,2]{2,1,0:T(1,128)} %bitcast), calls=%async_computation | async-start | bytes 32768 | tf_op jit(solution)/shard_map/all_to_all | solution.py:84
  18.5 119.6 %all-gather.5.cloned.1.call-start = ((), (), s32[]{:S(2)}) async-start(), calls=%async_computation.4 | async-start | bytes 5160960 | tf_op jit(solution)/shard_map/all_gather | solution.py:100
  78.1 5.8 %copy-start.15 = (f32[3,896]{1,0:T(4,128)S(1)}, f32[3,896]{1,0:T(4,128)}, u32[]{:S(2)}) copy-start(f32[3,896]{1,0:T(4,128)} %param.13) | copy-start | bytes 32260
  79.0 5.0 copy-start.8
  79.1 5.9 %collective-permute-start = (bf16[18,1,896]{2,1,0:T(2,128)(2,1)S(1)}, bf16[18,1,896]{2,1,0:T(2,128)(2,1)S(1)}, u32[]{:S(2)}, u32[]{:S(2)}) collective-permute-start(bf16[18,1,896]{2,1,0:T(2,128)(2,1)S(1)} %get-tuple-element.41), channel_id=1, source_target_pairs={{0,1},{1,2},{2,3},{4,5},{5,6},{6,7},{8,9},{9,10},{10,11},{12,13},{... | collective-permute-start | bytes 96776 | tf_op jit(solution)/shard_map/ppermute | solution.py:20
  82.6 6.6 %collective-permute-start.1 = (bf16[18,1,896]{2,1,0:T(2,128)(2,1)S(1)}, bf16[18,1,896]{2,1,0:T(2,128)(2,1)S(1)}, u32[]{:S(2)}, u32[]{:S(2)}) collective-permute-start(bf16[18,1,896]{2,1,0:T(2,128)(2,1)S(1)} %get-tuple-element.42), channel_id=1, source_target_pairs={{1,0},{2,1},{3,2},{5,4},{6,5},{7,6},{9,8},{10,9},{11,10},{13,12},{... | collective-permute-start | bytes 96776 | tf_op jit(solution)/shard_map/ppermute | solution.py:23
  84.1 5.2 copy-start.6
  91.1 203.2 %reduce-scatter.2.cloned.1.call-start = ((), (), s32[]{:S(2)}) async-start(), calls=%async_computation.5 | async-start | bytes 10321920 | tf_op jit(solution)/shard_map/reduce_scatter | solution.py:146
  145.6 2.2 copy-start.16
  145.6 2.7 copy-start.17
  148.3 8.8 %copy-start.2 = (bf16[288,8,8,128]{3,2,1,0:T(8,128)(2,1)}, bf16[288,8,8,128]{3,2,1,0:T(8,128)(2,1)S(1)}, u32[]{:S(2)}) copy-start(bf16[288,8,8,128]{3,2,1,0:T(8,128)(2,1)S(1)} %copy.80) | copy-start | bytes 14155780
  158.9 3.6 copy-start.5
  178.2 5.8 %copy-start.4 = (f32[9,8,64,256]{3,2,1,0:T(8,128)S(1)}, f32[9,8,64,256]{3,2,1,0:T(8,128)}, u32[]{:S(2)}) copy-start(f32[9,8,64,256]{3,2,1,0:T(8,128)} %get-tuple-element.44) | copy-start | bytes 14155780
  178.2 5.8 %copy-start.14 = (bf16[72,8,8,128]{3,2,1,0:T(8,128)(2,1)S(1)}, bf16[72,8,8,128]{3,2,1,0:T(8,128)(2,1)}, u32[]{:S(2)}) copy-start(bf16[72,8,8,128]{3,2,1,0:T(8,128)(2,1)} %copy.84) | copy-start | bytes 3538948
  183.9 21.0 %copy-start.10 = (bf16[9,256,8,128]{3,2,1,0:T(8,128)(2,1)}, bf16[9,256,8,128]{3,2,1,0:T(8,128)(2,1)S(1)}, u32[]{:S(2)}) copy-start(bf16[9,256,8,128]{3,2,1,0:T(8,128)(2,1)S(1)} %copy.72) | copy-start | bytes 14155780
  191.3 1.4 copy-start.3
  197.6 7.3 %copy-start.11 = (bf16[9,256,8,128]{3,2,1,0:T(8,128)(2,1)}, bf16[9,256,8,128]{3,2,1,0:T(8,128)(2,1)S(1)}, u32[]{:S(2)}) copy-start(bf16[9,256,8,128]{3,2,1,0:T(8,128)(2,1)S(1)} %copy.70) | copy-start | bytes 14155780
  197.7 7.3 %copy-start.18 = (bf16[896,1024]{1,0:T(8,128)(2,1)S(1)}, bf16[896,1024]{1,0:T(8,128)(2,1)}, u32[]{:S(2)}) copy-start(bf16[896,1024]{1,0:T(8,128)(2,1)} %param.12) | copy-start | bytes 5505028
  214.4 89.0 %copy-start.7 = (bf16[18,32,896]{2,1,0:T(8,128)(2,1)S(1)}, bf16[18,32,896]{2,1,0:T(8,128)(2,1)}, u32[]{:S(2)}) copy-start(bf16[18,32,896]{2,1,0:T(8,128)(2,1)} %copy-done.6) | copy-start | bytes 3096580
  214.4 89.0 %copy-start.9 = (bf16[3,8,32,896]{3,2,1,0:T(8,128)(2,1)S(1)}, bf16[3,8,32,896]{3,2,1,0:T(8,128)(2,1)}, u32[]{:S(2)}) copy-start(bf16[3,8,32,896]{3,2,1,0:T(8,128)(2,1)} %copy-done.8) | copy-start | bytes 4128772
  214.4 181.9 %all-gather.7.cloned.1.call-start = ((), (), s32[]{:S(2)}) async-start(), calls=%async_computation.6 | async-start | bytes 1849344 | tf_op jit(solution)/shard_map/all_gather | solution.py:167
  295.6 6.1 %collective-permute-start.2 = (f32[18,1,896]{2,1,0:T(1,128)S(1)}, f32[18,1,896]{2,1,0:T(1,128)S(1)}, u32[]{:S(2)}, u32[]{:S(2)}) collective-permute-start(f32[18,1,896]{2,1,0:T(1,128)S(1)} %get-tuple-element.39), channel_id=1, source_target_pairs={{1,0},{2,1},{3,2},{5,4},{6,5},{7,6},{9,8},{10,9},{11,10},{13,12},{... | collective-permute-start | bytes 193544 | tf_op jit(solution)/shard_map/ppermute | solution.py:23
  296.9 6.4 %collective-permute-start.3 = (f32[18,1,896]{2,1,0:T(1,128)S(1)}, f32[18,1,896]{2,1,0:T(1,128)S(1)}, u32[]{:S(2)}, u32[]{:S(2)}) collective-permute-start(f32[18,1,896]{2,1,0:T(1,128)S(1)} %get-tuple-element.40), channel_id=1, source_target_pairs={{0,1},{1,2},{2,3},{4,5},{5,6},{6,7},{8,9},{9,10},{10,11},{12,13},{... | collective-permute-start | bytes 193544 | tf_op jit(solution)/shard_map/ppermute | solution.py:20
  310.4 10.0 %copy-start.12 = (bf16[18,32,896]{2,1,0:T(8,128)(2,1)S(1)}, bf16[18,32,896]{2,1,0:T(8,128)(2,1)}, u32[]{:S(2)}) copy-start(bf16[18,32,896]{2,1,0:T(8,128)(2,1)} %get-tuple-element.38) | copy-start | bytes 3096580
  324.6 74.1 %all-to-all-start.2 = ((bf16[32,2,32,896]{3,2,1,0:T(8,128)(2,1)}), bf16[32,2,32,896]{3,2,1,0:T(8,128)(2,1)}, u32[]{:S(2)}, u32[]{:S(2)}) async-start(bf16[32,2,32,896]{3,2,1,0:T(8,128)(2,1)} %bitcast.132), calls=%async_computation.3 | async-start | bytes 7340032 | tf_op jit(solution)/shard_map/all_to_all | solution.py:155
  332.2 186.7 %all-reduce.3.cloned.1.call-start = ((), (), s32[]{:S(2)}) async-start(), calls=%async_computation.7 | async-start | bytes 14680064 | tf_op jit(solution)/shard_map/psum | solution.py:166
  518.9 4.5 copy-start.13
  518.9 6.4 %copy-start.1 = (bf16[896,1024]{1,0:T(8,128)(2,1)S(1)}, bf16[896,1024]{1,0:T(8,128)(2,1)}, u32[]{:S(2)}) copy-start(bf16[896,1024]{1,0:T(8,128)(2,1)} %param.11) | copy-start | bytes 5505028
Sparse Core Ops, SparseCore 0:
  91.2 46.8 all-gather.4
  214.6 79.7 reduce-scatter.1
  310.5 85.7 all-gather.6
  400.6 118.1 all-reduce.2
